TPU v7x, 256 devices: a whole 4x4x8 slice. The times are simulated.
256 devices in a mesh: lat: 32 (over x_lo, z, core), lon: 8 (over x_hi, y).
Axes of the slice: x: 4 (x_hi: 2, x_lo: 2; x = x_hi * 2 + x_lo), y: 4, z: 8, core: 2. Of those that a mesh axis runs over, the one named last changes fastest.
Arguments:
- ocean_state: bfloat16 [256, 1024, 384], P('lat', 'lon'), may hold values from -6 to 6
- kernel: float32 [49, 384], replicated, may hold values from -0.875 to 0.875
- norm_gain: float32 [384], replicated, may hold values from 0.5 to 1.5
- weight_in: bfloat16 [384, 1536], P('lat'), may hold values from -0.3125 to 0.3125
- weight_out: bfloat16 [1536, 384], P('lat'), may hold values from -0.15625 to 0.15625
- layer_scale: float32 [384], replicated, may hold values from 0.5 to 1.5
- cotangent: bfloat16 [256, 1024, 384], P('lat', 'lon'), may hold values from -6 to 6
- tile_list: int32 [32, 8, 6], P('lat', 'lon'), may hold values from 0 to 7, as said below
- ocean_count: int32 [32, 8], P('lat', 'lon'), may hold values from 1 to 6, as said below
Outputs:
- new_state: bfloat16 [256, 1024, 384], P('lat', 'lon')
- grad_state: bfloat16 [256, 1024, 384], P('lat', 'lon')
- grad_weight_in: float32 [384, 1536], P('lat')
- grad_weight_out: float32 [1536, 384], P('lat')
- grad_kernel: float32 [49, 384], replicated
Inputs may be any that keep to these rules, and one draw needn't show every extreme that they name: `tile_list`: for each device, 6 distinct tile numbers of its own block; the first ocean_count of them are its ocean tiles, the others are land tiles. `ocean_count`: ocean tiles of each device; some device has exactly 6.
All inputs are finite; a program needn't handle non-finite values.
Results may differ from a plain program's by a relative error of at most 0.0062.
Values may be sent and summed in bfloat16 or wider, within the bound.
A program may use at most 128 MiB of HBM per device.

v0:
```python
import math

import jax
import jax.numpy as jnp
from jax import lax
from jax.sharding import PartitionSpec as P

TAPS = 7
TILE = 128
REACH = 3
TILES_DEV = 8


EPS = 1e-06
ROOT_HALF = 0.7071067811865476
INV_ROOT_TWO_PI = 0.3989422804014327


def padded_2(shard, sides, width, wrap):
    for axis, dim in sides:
        peers, length = (lax.axis_size(axis), shard.shape[dim])
        up = [(i, (i + 1) % peers) for i in range(peers if wrap else peers - 1)]
        down = [(j, i) for i, j in up]
        last = lax.slice_in_dim(shard, length - width, length, axis=dim)
        leading = lax.slice_in_dim(shard, 0, width, axis=dim)
        before = lax.ppermute(last, axis, up)
        after = lax.ppermute(leading, axis, down)
        shard = jnp.concatenate([before, shard, after], axis=dim)
    return shard


def gelu_value(hidden):
    return 0.5 * hidden * (1.0 + lax.erf(hidden * ROOT_HALF))


def gelu_slope(hidden):
    return 0.5 * (1.0 + lax.erf(hidden * ROOT_HALF)) + hidden * INV_ROOT_TWO_PI * jnp.exp(
        -0.5 * hidden * hidden
    )


def ocean_cells(tile_list, ocean_count):
    slot_ids = jnp.arange(tile_list.shape[-1], dtype=jnp.int32)
    live_slots = slot_ids < ocean_count[..., None]
    tile_ids = jnp.arange(TILES_DEV, dtype=jnp.int32)
    matches = (tile_list[..., None] == tile_ids) & live_slots[..., None]
    return jnp.any(matches, axis=-2).astype(jnp.float32)


def stencil(padded, kernel, height, breadth, flipped):
    summed = jnp.zeros((height, breadth, padded.shape[-1]), jnp.float32)
    for row_tap in range(TAPS):
        for col_tap in range(TAPS):
            if flipped:
                row_from = 2 * REACH - row_tap
                col_from = 2 * REACH - col_tap
            else:
                row_from = row_tap
                col_from = col_tap
            window = padded[row_from : row_from + height, col_from : col_from + breadth]
            summed = summed + kernel[row_tap * TAPS + col_tap] * window.astype(jnp.float32)
    return summed


def kernel_terms(padded, grad_conv, height, breadth):
    rows_out = []
    for row_tap in range(TAPS):
        for col_tap in range(TAPS):
            window = padded[row_tap : row_tap + height, col_tap : col_tap + breadth].astype(
                jnp.float32
            )
            rows_out.append(jnp.sum(window * grad_conv, axis=(0, 1)))
    return jnp.stack(rows_out)


def extend(block):
    taller = padded_2(block, (("lat", 0),), REACH, False)
    return padded_2(taller, (("lon", 1),), REACH, True)


def contract_rows(left, right):
    return lax.dot_general(
        left, right, (((0,), (0,)), ((), ())), preferred_element_type=jnp.float32
    )


def contract_cols(left, right):
    return lax.dot_general(
        left, right, (((1,), (1,)), ((), ())), preferred_element_type=jnp.float32
    )


def pointwise(conv_rows, cot_rows, live_rows, norm_gain, layer_scale, full_in, full_out):
    centre = conv_rows - jnp.mean(conv_rows, axis=-1, keepdims=True)
    spread = lax.rsqrt(jnp.mean(centre * centre, axis=-1, keepdims=True) + EPS)
    unit_rows = centre * spread
    normed = (unit_rows * norm_gain).astype(jnp.bfloat16)
    hidden = jnp.dot(normed, full_in, preferred_element_type=jnp.float32)
    active = gelu_value(hidden).astype(jnp.bfloat16)
    mixed_rows = jnp.dot(active, full_out, preferred_element_type=jnp.float32)
    grad_mixed = (live_rows * layer_scale * cot_rows.astype(jnp.float32)).astype(jnp.bfloat16)
    part_out = contract_rows(active, grad_mixed)
    grad_active = contract_cols(grad_mixed, full_out)
    grad_hidden = (grad_active * gelu_slope(hidden)).astype(jnp.bfloat16)
    part_in = contract_rows(normed, grad_hidden)
    grad_normed = contract_cols(grad_hidden, full_in)
    grad_unit = grad_normed * norm_gain
    grad_conv = spread * (
        grad_unit
        - jnp.mean(grad_unit, axis=-1, keepdims=True)
        - unit_rows * jnp.mean(grad_unit * unit_rows, axis=-1, keepdims=True)
    )
    return (mixed_rows, grad_conv, part_in, part_out)


def per_device(
    ocean_state,
    kernel,
    norm_gain,
    weight_in,
    weight_out,
    layer_scale,
    cotangent,
    tile_list,
    ocean_count,
):
    height, breadth, channels = ocean_state.shape
    full_in, full_out = (
        lax.all_gather(weight_in, "lat", axis=0, tiled=True),
        lax.all_gather(weight_out, "lat", axis=0, tiled=True),
    )
    extended = extend(ocean_state)
    conv_field = stencil(extended, kernel, height, breadth, False)
    flags = ocean_cells(tile_list, ocean_count).reshape(height, breadth // TILE)
    live_rows = jnp.repeat(flags, TILE, axis=1).reshape(-1, 1)
    mixed_rows, grad_conv, part_in, part_out = pointwise(
        conv_field.reshape(-1, channels),
        cotangent.reshape(-1, channels),
        live_rows,
        norm_gain,
        layer_scale,
        full_in,
        full_out,
    )
    branch_term = (live_rows * layer_scale * mixed_rows).reshape(height, breadth, channels)
    new_state = (ocean_state.astype(jnp.float32) + branch_term).astype(jnp.bfloat16)
    grad_conv = grad_conv.reshape(height, breadth, channels)
    part_kernel = kernel_terms(extended, grad_conv, height, breadth)
    sum_in, sum_out, sum_kernel = lax.psum((part_in, part_out, part_kernel), ("lat", "lon"))
    band_id = lax.axis_index("lat")
    sum_in = lax.dynamic_slice_in_dim(sum_in, band_id * weight_in.shape[0], weight_in.shape[0], 0)
    sum_out = lax.dynamic_slice_in_dim(
        sum_out, band_id * weight_out.shape[0], weight_out.shape[0], 0
    )
    grad_half = grad_conv.astype(jnp.bfloat16)
    spread_back = stencil(extend(grad_half), kernel, height, breadth, True)
    grad_state = (cotangent.astype(jnp.float32) + spread_back).astype(jnp.bfloat16)
    norm_factor = 1.0 / math.sqrt(height * breadth * lax.axis_size("lat") * lax.axis_size("lon"))
    return (
        new_state,
        grad_state,
        sum_in * norm_factor,
        sum_out * norm_factor,
        sum_kernel * norm_factor,
    )


def solution(mesh):
    return jax.shard_map(
        per_device,
        mesh=mesh,
        in_specs=(
            P("lat", "lon", None),
            P(),
            P(),
            P("lat", None),
            P("lat", None),
            P(),
            P("lat", "lon", None),
            P("lat", "lon", None),
            P("lat", "lon"),
        ),
        out_specs=(
            P("lat", "lon", None),
            P("lat", "lon", None),
            P("lat", None),
            P("lat", None),
            P(),
        ),
        check_vma=False,
    )
```

profile of v0, /device:TPU:32, one launch (start us, length us, event | category | flops | bytes accessed | tf_op | source)
XLA Modules:
  0.0 478.6 jit_solution(1076435762413053982)
XLA Ops:
  11.7 3.7 collective-permute-start.1
  27.6 4.1 collective-permute-start.3
  34.0 20.6 %fusion.153 = (f32[8,128]{1,0:T(8,128)S(1)}, f32[8,128,384]{2,1,0:T(8,128)S(1)}) fusion(bf16[14,3,384]{2,1,0:T(4,128)(2,1)} %collective-permute-done.3, bf16[14,128,384]{2,1,0:T(8,128)(2,1)S(1)} %get-tuple-element.133, f32[384]{0:T(512)} %get-tuple-element.109, f32[384]{0:T(512)} %get-tuple-element.110, f32[384]{0:T(512)S(1)} %get-tuple-element.63, ...), kind=kLoop, calls=%fused_computation.386 | loop fusion | flops 107346944 | bytes 8598016 | tf_op jit(solution)/shard_map/reduce_sum | solution.py:94
  57.0 19.1 %all-gather.6.cloned.1.call-done = bf16[32,12,1536]{2,1,0:T(8,128)(2,1)} async-done(((bf16[1,12,1536]{2,1,0:T(8,128)(2,1)}), bf16[32,12,1536]{2,1,0:T(8,128)(2,1)}) %all-gather.6.cloned.1.call-update) | async-done | bytes 1179664 | tf_op jit(solution)/shard_map/all_gather | solution.py:129
  76.0 3.0 reshape.200
  79.0 5.9 %multiply_convert_fusion = (bf16[1024,1536]{1,0:T(8,128)(2,1)}, f32[1024,1536]{1,0:T(8,128)}) fusion(bf16[1024,384]{1,0:T(8,128)(2,1)} %multiply_convert_fusion.1, bf16[384,1536]{1,0:T(8,128)(2,1)} %reshape.200), kind=kOutput, calls=%fused_computation.46 | convolution fusion | flops 1215823872 | bytes 11403264 | tf_op jit(solution)/shard_map/dot_general | solution.py:98
  85.0 56.4 %all-gather.4.cloned.1.call-done = bf16[1536,384]{1,0:T(8,128)(2,1)} async-done(((bf16[48,384]{1,0:T(8,128)(2,1)}), bf16[1536,384]{1,0:T(8,128)(2,1)}) %all-gather.4.cloned.1.call-update) | async-done | bytes 1179664 | tf_op jit(solution)/shard_map/all_gather | solution.py:130
  141.4 5.5 %fusion.4 = bf16[1024,1536]{1,0:T(8,128)(2,1)S(1)} fusion(f32[1024,1536]{1,0:T(8,128)} %get-tuple-element.137, bf16[1024,384]{1,0:T(8,128)(2,1)} %fusion.101, bf16[1536,384]{1,0:T(8,128)(2,1)} %all-gather.4.cloned.1.call-done), kind=kOutput, calls=%fused_computation.45 | convolution fusion | flops 1223688192 | bytes 11403264 | tf_op jit(solution)/shard_map/dot_general | solution.py:88
  146.9 2.0 fusion.152
  148.9 2.8 fusion.158
  151.8 3.2 fusion.159
  155.0 3.5 fusion.93
  158.7 2.2 collective-permute-start.4
  160.9 3.6 collective-permute-start.5
  164.5 2.8 fusion.98
  167.3 2.5 fusion.94
  169.8 2.9 fusion.99
  172.7 2.5 fusion.95
  175.2 2.9 fusion.100
  178.2 2.4 fusion.96
  183.3 5.2 %collective-permute-start.6 = (bf16[14,3,384]{2,1,0:T(4,128)(2,1)S(1)}, bf16[14,3,384]{2,1,0:T(4,128)(2,1)S(1)}, u32[]{:S(2)}, u32[]{:S(2)}) collective-permute-start(bf16[14,3,384]{2,1,0:T(4,128)(2,1)S(1)} %get-tuple-element.119), channel_id=1, source_target_pairs={{1,0},{2,1},{3,2},{4,3},{5,4},{6,5},{7,6},{0,7},{9,8},{10,9},{11,1... | collective-permute-start | bytes 96776 | tf_op jit(solution)/shard_map/ppermute | solution.py:27
  190.2 4.4 stack.199
  198.5 17.0 %add_convert_fusion = bf16[8,128,384]{2,1,0:T(8,128)(2,1)} fusion(bf16[8,128,384]{2,1,0:T(8,128)(2,1)S(1)} %copy-done.3, bf16[3,128,384]{2,1,0:T(8,128)(2,1)S(1)} %copy-done.11, bf16[3,128,384]{2,1,0:T(8,128)(2,1)S(1)} %copy-done.13, bf16[14,131,384]{2,1,0:T(8,128)(2,1)S(1)} %get-tuple-element.118, bf16[14,131,384]{2,1,0:T(8,128)(2,1)S(1)} %get-tuple-element.117, ...), kind=kLoop, calls=%fused_computation.250 | loop fusion | flops 60948480 | bytes 36054528 | tf_op jit(solution)/shard_map/convert_element_type | solution.py:157
  215.5 251.9 %all-reduce.3.cloned.1.call-done = (f32[384,1536]{1,0:T(8,128)}, f32[1536,384]{1,0:T(8,128)}, f32[49,384]{1,0:T(8,128)}) async-done(((f32[384,1536]{1,0:T(8,128)}, f32[1536,384]{1,0:T(8,128)}, f32[49,384]{1,0:T(8,128)}), (f32[384,1536]{1,0:T(8,128)}, f32[1536,384]{1,0:T(8,128)}, f32[49,384]{1,0:T(8,128)})) %all-reduce.3.cloned.1.call-update) | async-done | bytes 4793872 | tf_op jit(solution)/shard_map/psum | solution.py:149
  (212 shorter events, 32.7 us)
Async XLA Ops:
  7.2 13.6 %copy-start.8 = (bf16[8,128,384]{2,1,0:T(8,128)(2,1)S(1)}, bf16[8,128,384]{2,1,0:T(8,128)(2,1)}, u32[]{:S(2)}) copy-start(bf16[8,128,384]{2,1,0:T(8,128)(2,1)} %param.15) | copy-start | bytes 2359300
  7.2 68.8 %all-gather.6.cloned.1.call-start = ((), (), s32[]{:S(2)}) async-start(), calls=%async_computation.1 | async-start | bytes 1622016 | tf_op jit(solution)/shard_map/all_gather | solution.py:129
  7.9 133.5 %all-gather.4.cloned.1.call-start = ((), (), s32[]{:S(2)}) async-start(), calls=%async_computation | async-start | bytes 1216512 | tf_op jit(solution)/shard_map/all_gather | solution.py:130
  9.8 12.8 %collective-permute-start = (bf16[3,128,384]{2,1,0:T(8,128)(2,1)S(1)}, bf16[3,128,384]{2,1,0:T(8,128)(2,1)S(1)}, u32[]{:S(2)}, u32[]{:S(2)}) collective-permute-start(bf16[3,128,384]{2,1,0:T(8,128)(2,1)S(1)} %get-tuple-element.129), channel_id=1, source_target_pairs={{0,8},{8,16},{16,24},{24,32},{32,40},{40,48},{48,56},{56,64},{64,7... | collective-permute-start | bytes 884744 | tf_op jit(solution)/shard_map/ppermute | solution.py:26
  11.7 12.6 %collective-permute-start.1 = (bf16[3,128,384]{2,1,0:T(8,128)(2,1)}, bf16[3,128,384]{2,1,0:T(8,128)(2,1)}, u32[]{:S(2)}, u32[]{:S(2)}) collective-permute-start(bf16[3,128,384]{2,1,0:T(8,128)(2,1)} %get-tuple-element.128), channel_id=1, source_target_pairs={{8,0},{16,8},{24,16},{32,24},{40,32},{48,40},{56,48},{64,56},{72,6... | collective-permute-start | bytes 884744 | tf_op jit(solution)/shard_map/ppermute | solution.py:27
  15.4 452.0 %all-reduce.3.cloned.1.call-start = ((), (), s32[]{:S(2)}) async-start(), calls=%async_computation.2 | async-start | bytes 9609216 | tf_op jit(solution)/shard_map/psum | solution.py:149
  17.4 16.6 %copy-start.15 = (f32[384]{0:T(512)}, f32[384]{0:T(512)S(1)}, u32[]{:S(2)}) copy-start(f32[384]{0:T(512)S(1)} %get-tuple-element.64) | copy-start | bytes 4612
  17.4 16.6 %copy-start.17 = (f32[384]{0:T(512)}, f32[384]{0:T(512)S(1)}, u32[]{:S(2)}) copy-start(f32[384]{0:T(512)S(1)} %get-tuple-element.65) | copy-start | bytes 4612
  26.0 8.0 %collective-permute-start.2 = (bf16[14,3,384]{2,1,0:T(4,128)(2,1)}, bf16[14,3,384]{2,1,0:T(4,128)(2,1)}, u32[]{:S(2)}, u32[]{:S(2)}) collective-permute-start(bf16[14,3,384]{2,1,0:T(4,128)(2,1)} %get-tuple-element.121), channel_id=1, source_target_pairs={{0,1},{1,2},{2,3},{3,4},{4,5},{5,6},{6,7},{7,0},{8,9},{9,10},{10,1... | collective-permute-start | bytes 96776 | tf_op jit(solution)/shard_map/ppermute | solution.py:26
  27.6 6.4 %collective-permute-start.3 = (bf16[14,3,384]{2,1,0:T(4,128)(2,1)}, bf16[14,3,384]{2,1,0:T(4,128)(2,1)}, u32[]{:S(2)}, u32[]{:S(2)}) collective-permute-start(bf16[14,3,384]{2,1,0:T(4,128)(2,1)} %get-tuple-element.122), channel_id=1, source_target_pairs={{1,0},{2,1},{3,2},{4,3},{5,4},{6,5},{7,6},{0,7},{9,8},{10,9},{11,1... | collective-permute-start | bytes 96776 | tf_op jit(solution)/shard_map/ppermute | solution.py:27
  141.4 5.5 %copy-start.1 = (f32[8,128,384]{2,1,0:T(8,128)S(1)}, f32[8,128,384]{2,1,0:T(8,128)}, u32[]{:S(2)}) copy-start(f32[8,128,384]{2,1,0:T(8,128)} %copy-done) | copy-start | bytes 4718596
  141.4 5.5 %copy-start.7 = (bf16[384,1536]{1,0:T(8,128)(2,1)S(1)}, bf16[384,1536]{1,0:T(8,128)(2,1)}, u32[]{:S(2)}) copy-start(bf16[384,1536]{1,0:T(8,128)(2,1)} %reshape.200) | copy-start | bytes 3538948
  141.4 5.5 %copy-start.57 = (f32[384]{0:T(512)S(1)}, f32[384]{0:T(512)}, u32[]{:S(2)}) copy-start(f32[384]{0:T(512)} %param.11) | copy-start | bytes 4612
  158.6 24.6 %copy-start.2 = (bf16[8,128,384]{2,1,0:T(8,128)(2,1)}, bf16[8,128,384]{2,1,0:T(8,128)(2,1)S(1)}, u32[]{:S(2)}) copy-start(bf16[8,128,384]{2,1,0:T(8,128)(2,1)S(1)} %convert_element_type.439) | copy-start | bytes 2359300
  158.7 24.5 %collective-permute-start.4 = (bf16[3,128,384]{2,1,0:T(8,128)(2,1)S(1)}, bf16[3,128,384]{2,1,0:T(8,128)(2,1)S(1)}, u32[]{:S(2)}, u32[]{:S(2)}) collective-permute-start(bf16[3,128,384]{2,1,0:T(8,128)(2,1)S(1)} %get-tuple-element.124), channel_id=1, source_target_pairs={{0,8},{8,16},{16,24},{24,32},{32,40},{40,48},{48,56},{56,64},{64,7... | collective-permute-start | bytes 884744 | tf_op jit(solution)/shard_map/ppermute | solution.py:26
  160.9 22.4 %collective-permute-start.5 = (bf16[3,128,384]{2,1,0:T(8,128)(2,1)S(1)}, bf16[3,128,384]{2,1,0:T(8,128)(2,1)S(1)}, u32[]{:S(2)}, u32[]{:S(2)}) collective-permute-start(bf16[3,128,384]{2,1,0:T(8,128)(2,1)S(1)} %get-tuple-element.123), channel_id=1, source_target_pairs={{8,0},{16,8},{24,16},{32,24},{40,32},{48,40},{56,48},{64,56},{72,6... | collective-permute-start | bytes 884744 | tf_op jit(solution)/shard_map/ppermute | solution.py:27
  183.2 6.4 %copy-start.10 = (bf16[3,128,384]{2,1,0:T(8,128)(2,1)}, bf16[3,128,384]{2,1,0:T(8,128)(2,1)S(1)}, u32[]{:S(2)}) copy-start(bf16[3,128,384]{2,1,0:T(8,128)(2,1)S(1)} %collective-permute-done.4) | copy-start | bytes 884740
  183.3 6.4 %copy-start.12 = (bf16[3,128,384]{2,1,0:T(8,128)(2,1)}, bf16[3,128,384]{2,1,0:T(8,128)(2,1)S(1)}, u32[]{:S(2)}) copy-start(bf16[3,128,384]{2,1,0:T(8,128)(2,1)S(1)} %collective-permute-done.5) | copy-start | bytes 884740
  183.3 11.6 %collective-permute-start.6 = (bf16[14,3,384]{2,1,0:T(4,128)(2,1)S(1)}, bf16[14,3,384]{2,1,0:T(4,128)(2,1)S(1)}, u32[]{:S(2)}, u32[]{:S(2)}) collective-permute-start(bf16[14,3,384]{2,1,0:T(4,128)(2,1)S(1)} %get-tuple-element.119), channel_id=1, source_target_pairs={{1,0},{2,1},{3,2},{4,3},{5,4},{6,5},{7,6},{0,7},{9,8},{10,9},{11,1... | collective-permute-start | bytes 96776 | tf_op jit(solution)/shard_map/ppermute | solution.py:27
  188.6 7.6 %collective-permute-start.7 = (bf16[14,3,384]{2,1,0:T(4,128)(2,1)S(1)}, bf16[14,3,384]{2,1,0:T(4,128)(2,1)S(1)}, u32[]{:S(2)}, u32[]{:S(2)}) collective-permute-start(bf16[14,3,384]{2,1,0:T(4,128)(2,1)S(1)} %get-tuple-element.120), channel_id=1, source_target_pairs={{0,1},{1,2},{2,3},{3,4},{4,5},{5,6},{6,7},{7,0},{8,9},{9,10},{10,1... | collective-permute-start | bytes 96776 | tf_op jit(solution)/shard_map/ppermute | solution.py:26
  194.6 3.6 copy-start.9
  194.6 3.5 copy-start.16
  194.6 3.5 copy-start.18
  194.6 3.5 copy-start.19
  (46 other events, 144.0 us)
Sparse Core Ops, SparseCore 0:
  9.9 66.1 all-gather.5
  77.9 63.4 all-gather.3
  194.7 272.6 all-reduce.2
where the time goes:
time: 482 us; the launch traced here: 479 us
  waiting for transfers between devices  330 us (68%)
  other arithmetic  69.8 us (14%)
  starting transfers between devices  22.3 us (5%)
  matrix products  21.3 us (4%)
  local copies, waits for them, and re-layouts  19.3 us (4%)
  between operations  15.8 us (3%)
    psum x1, waiting for transfers between devices, per_device(): lax.psum((part_in, part_out, part_kernel), ('lat', 'lon'))  252 us
    all_gather x1, waiting for transfers between devices, per_device(): lax.all_gather(weight_out, 'lat', axis=0, tiled=True)  56.4 us
    reduce_sum x1, other arithmetic, pointwise(): centre = conv_rows - jnp.mean(conv_rows, axis=-1, keepdims=True)  20.6 us
    reduce_sum x8, other arithmetic, kernel_terms(): rows_out.append(jnp.sum(window * grad_conv, axis=(0, 1)))  20.3 us
    all_gather x1, waiting for transfers between devices, per_device(): lax.all_gather(weight_in, 'lat', axis=0, tiled=True)  19.1 us
    convert_element_type x1, other arithmetic, per_device(): (cotangent.astype(jnp.float32) + spread_back).astype(jnp.bfloat16)  17 us
    ppermute x4, starting transfers between devices, padded_2(): after = lax.ppermute(leading, axis, down)  16.6 us
  transfers between devices with their start and end apart: 11, of which 5 were waited for; matrix products, arithmetic and copies ran while one was open for 18% of the time, Pallas kernels for 0%

commit v1 on v0

v1 whole, which is shorter than its diff:
```python
import functools
import math

import jax
import jax.numpy as jnp
from jax import lax
from jax.experimental import pallas as pl
from jax.experimental.pallas import tpu as pltpu
from jax.sharding import PartitionSpec as P

TAPS = 7
REACH = 3
ROWS = 8
COLS = 128
C = 384
FF = 1536
NZ = 8
NY = 4
NX = 4
EPS = 1e-06
ROOT_HALF = 0.7071067811865476
INV_ROOT_TWO_PI = 0.3989422804014327
BF = jnp.bfloat16
F32 = jnp.float32
MESH = pl.DeviceIdType.MESH
N_SEM = 128


def gelu_pair(h):
    cdf = 0.5 * (1.0 + lax.erf(h * ROOT_HALF))
    return h * cdf, cdf + h * (INV_ROOT_TWO_PI * jnp.exp(-0.5 * h * h))


def nt(left, right):
    return lax.dot_general(left, right, (((1,), (1,)), ((), ())), preferred_element_type=F32)


def tn(left, right):
    return lax.dot_general(left, right, (((0,), (0,)), ((), ())), preferred_element_type=F32)


def nn(left, right):
    return jnp.dot(left, right, preferred_element_type=F32)


class Copy:
    def __init__(self, sems, src, dst, dev, land=None, send_if=None, recv_if=None):
        send, recv, counter = sems
        self.slot = counter[0]
        counter[0] += 1
        self.send_sem, self.recv_sem = send.at[self.slot], recv.at[self.slot]
        self.src, self.dst, self.dev = src, dst, dev
        self.land = dst if land is None else land
        self.send_if, self.recv_if = send_if, recv_if

    def _make(self, dst):
        return pltpu.make_async_remote_copy(
            src_ref=self.src,
            dst_ref=dst,
            send_sem=self.send_sem,
            recv_sem=self.recv_sem,
            device_id=self.dev,
            device_id_type=MESH,
        )

    def start(self):
        if self.send_if is None:
            self._make(self.dst).start()
        else:
            pl.when(self.send_if)(lambda: self._make(self.dst).start())

    def arrived(self):
        if self.recv_if is None:
            self._make(self.land).wait_recv()
        else:
            pl.when(self.recv_if)(lambda: self._make(self.land).wait_recv())

    def left(self):
        if self.send_if is None:
            self._make(self.dst).wait_send()
        else:
            pl.when(self.send_if)(lambda: self._make(self.dst).wait_send())


def kernel_body(
    tile_ref, count_ref, x_ref, k_ref, gain_ref, win_ref, wout_ref, scale_ref, cot_ref,
    new_ref, gs_ref, gwi_ref, gwo_ref, gk_ref,
    hrow, hcol, hcor, ext, ext2, k8, conv, spread_b, normed, npt, gm, ghalf,
    gath, w_in, sel, act, slope, gh, mixed, gn,
    ro, ri, cpo, cpi, ypo, ypi, xpo, xpi, xro, xri, zpo, zpi, zro, zri, fo, fi,
    kp, kz, kc, kx, ky, kcs, kxs, kys, kf,
    send, recv,
):
    lat, lon = lax.axis_index("lat"), lax.axis_index("lon")
    core, z, xlo = lax.rem(lat, 2), lax.rem(lat // 2, NZ), lat // (2 * NZ)
    y, xhi = lax.rem(lon, NY), lon // NY
    x = xhi * 2 + xlo
    q = xlo * NZ + z
    sems = (send, recv, [0])

    def at(xx, zz, cc, yy):
        return ((lax.rem(xx, 2) * NZ + zz) * 2 + cc, (xx // 2) * NY + yy)

    def ring(v, k, n):
        return lax.rem(v + k + n, n)

    def zdev(k):
        return at(x, ring(z, k, NZ), core, y)

    def xdev(k):
        return at(ring(x, k, NX), z, core, y)

    def ydev(k):
        return at(x, z, core, ring(y, k, NY))

    other_core = at(x, z, 1 - core, y)

    def around(dr, dc):
        return (ring(lat, dr, 32), ring(lon, dc, 8))

    barrier = pltpu.get_barrier_semaphore()
    partners = [around(dr, dc) for dr in (-1, 0, 1) for dc in (-1, 0, 1) if dr or dc]
    partners += [zdev(k) for k in range(1, NZ)]
    partners += [xdev(k) for k in range(1, NX)]
    partners += [ydev(k) for k in range(1, NY)]
    partners += [other_core]
    for dev in partners:
        pl.semaphore_signal(barrier, inc=1, device_id=dev, device_id_type=MESH)

    gath[lat, 0:64, :] = jnp.zeros((64, C), BF)
    for j in range(4):
        gath[lat, 16 * j : 16 * j + 12, :] = win_ref[:, C * j : C * (j + 1)]
    gath[lat, 64:112, :] = wout_ref[...]
    pl.semaphore_wait(barrier, len(partners))

    started = []

    def begin(copies):
        for c in copies:
            c.start()
            started.append(c)

    def halo_copies(src, n):
        top, bottom = pl.ds(0, REACH), pl.ds(ROWS - REACH, REACH)
        first, last, every = pl.ds(0, 16), pl.ds(COLS - 16, 16), pl.ds(0, ROWS)
        out = [
            Copy(sems, src.at[bottom], hrow.at[n, 0], around(1, 0)),
            Copy(sems, src.at[top], hrow.at[n, 1], around(-1, 0)),
            Copy(sems, src.at[every, last], hcol.at[n, 0], around(0, 1)),
            Copy(sems, src.at[every, first], hcol.at[n, 1], around(0, -1)),
            Copy(sems, src.at[bottom, last], hcor.at[n, 0], around(1, 1)),
            Copy(sems, src.at[bottom, first], hcor.at[n, 1], around(1, -1)),
            Copy(sems, src.at[top, last], hcor.at[n, 2], around(-1, 1)),
            Copy(sems, src.at[top, first], hcor.at[n, 3], around(-1, -1)),
        ]
        return out

    halo1 = halo_copies(x_ref, 0)
    begin(halo1)

    def shard(xl, zz, cc):
        return (xl * NZ + zz) * 2 + cc

    offsets = [0, -1, 1, -2, 2, -3, 3, -4]
    olo = 1 - xlo
    zc = {}
    for o in offsets[1:]:
        s = shard(xlo, ring(z, o, NZ), core)
        step = 1 if o < 0 else -1
        hop = shard(xlo, ring(z, o + step, NZ), core)
        zc[o] = Copy(sems, gath.at[hop], gath.at[hop], zdev(step), land=gath.at[s])
    xc, cc1, cc2 = {}, {}, {}
    for i, o in enumerate(offsets):
        s = shard(xlo, ring(z, o, NZ), core)
        so = shard(olo, ring(z, o, NZ), core)
        xc[o] = Copy(sems, gath.at[s], gath.at[s], xdev(1 if i % 2 == 0 else -1), land=gath.at[so])
        cc1[o] = Copy(
            sems, gath.at[s], gath.at[s], other_core, land=gath.at[shard(xlo, ring(z, o, NZ), 1 - core)]
        )
        cc2[o] = Copy(
            sems, gath.at[so], gath.at[so], other_core, land=gath.at[shard(olo, ring(z, o, NZ), 1 - core)]
        )

    begin([zc[-1], zc[1], xc[0], cc1[0]])

    def ring_step(n):
        for o in (-n, n):
            if o not in zc:
                continue
            zc[o].arrived()
            onward = o - 1 if o < 0 else o + 1
            go = [zc[onward]] if onward in zc else []
            begin(go + [xc[o], cc1[o]])

    def cross_step(n):
        for o in (-n, n) if n else (0,):
            if o in xc:
                xc[o].arrived()
                begin([cc2[o]])

    flags = []
    for r in range(ROWS):
        hit = jnp.int32(0)
        for s in range(6):
            match = jnp.logical_and(tile_ref[0, 0, s] == r, s < count_ref[0, 0])
            hit = hit + jnp.where(match, 1, 0)
        flags.append(hit.astype(F32))
    for l in range(3):
        for t in range(TAPS * TAPS):
            k8[l, t] = jnp.broadcast_to(k_ref[t : t + 1, 128 * l : 128 * (l + 1)], (8, 128))
    gain = gain_ref[...]
    scale = scale_ref[...]
    for r in range(ROWS):
        row_scale = scale * flags[r]
        gm[pl.ds(COLS * r, COLS), :] = (row_scale * cot_ref[r].astype(F32)).astype(BF)

    def lanes(l):
        return pl.ds(pl.multiple_of(l * 128, 128), 128)

    def extend(src, n, dst):
        up_on = jnp.where(lat > 0, 1.0, 0.0).astype(F32)
        down_on = jnp.where(lat < 31, 1.0, 0.0).astype(F32)

        def put(row, mid, left, right, on):
            for l in range(3):
                sl = slice(128 * l, 128 * (l + 1))
                m, a, b = mid[:, sl].astype(F32), left[:, sl].astype(F32), right[:, sl].astype(F32)
                if on is not None:
                    m, a, b = m * on, a * on, b * on
                dst[l, row, 8 : 8 + COLS, :] = m
                dst[l, row, 0:8, :] = a[8:16]
                dst[l, row, 8 + COLS : 16 + COLS, :] = b[0:8]

        def middle(r, carry):
            put(REACH + r, src[r], hcol[n, 0, r], hcol[n, 1, r], None)
            return carry

        def above(r, carry):
            put(r, hrow[n, 0, r], hcor[n, 0, r], hcor[n, 1, r], up_on)
            return carry

        def below(r, carry):
            put(REACH + ROWS + r, hrow[n, 1, r], hcor[n, 2, r], hcor[n, 3, r], down_on)
            return carry

        lax.fori_loop(0, ROWS, middle, 0)
        lax.fori_loop(0, REACH, above, 0)
        lax.fori_loop(0, REACH, below, 0)

    def stencil(src, flipped, emit, first, last):
        def body(i, carry):
            l, cg = i // 16, lax.rem(i, 16)
            c0 = pl.multiple_of(cg * 8, 8)
            acc = [None] * ROWS
            for b in range(TAPS):
                rows = [src[l, row, pl.ds(c0 + 5 + b, 8), :] for row in range(ROWS + 2 * REACH)]
                for a in range(TAPS):
                    t = a * TAPS + b
                    tap = k8[l, TAPS * TAPS - 1 - t if flipped else t]
                    for r in range(ROWS):
                        term = tap * rows[r + a]
                        acc[r] = term if acc[r] is None else acc[r] + term
            for r in range(ROWS):
                emit(r, pl.ds(c0, 8), lanes(l), acc[r])
            return carry

        lax.fori_loop(first, last, body, 0)

    for c in halo1:
        c.arrived()
    extend(x_ref, 0, ext)
    ring_step(1)

    def emit_conv(r, cs, ls, v):
        conv[r, cs, ls] = v

    stencil(ext, False, emit_conv, 0, 16)
    ring_step(2)
    cross_step(0)
    stencil(ext, False, emit_conv, 16, 32)
    ring_step(3)
    cross_step(1)
    stencil(ext, False, emit_conv, 32, 48)
    ring_step(4)
    cross_step(2)

    def norm_row(r, carry):
        v = conv[r]
        centre = v - jnp.mean(v, axis=-1, keepdims=True)
        sp = lax.rsqrt(jnp.mean(centre * centre, axis=-1, keepdims=True) + EPS)
        unit = centre * sp
        conv[r] = unit
        spread_b[r] = jnp.broadcast_to(sp, (COLS, 128))
        normed[pl.ds(pl.multiple_of(r * COLS, COLS), COLS), :] = (unit * gain).astype(BF)
        return carry

    lax.fori_loop(0, ROWS, norm_row, 0)
    cross_step(3)
    cross_step(4)

    m = lax.broadcasted_iota(jnp.int32, (512, C), 0)
    ch = lax.broadcasted_iota(jnp.int32, (512, C), 1)
    blk, inside = lax.shift_right_logical(m, 4), jnp.bitwise_and(m, 15)
    src_shard = 2 * jnp.bitwise_and(blk, 15) + lax.shift_right_logical(blk, 4)
    pick = jnp.logical_and(inside < 12, ch == 12 * src_shard + inside)
    sel[...] = jnp.where(pick, 1.0, 0.0).astype(BF)

    def spread_t(i, carry):
        cells = pl.ds(pl.multiple_of(i * 256, 256), 256)
        npt[:, cells] = nt(sel[...], normed[cells, :]).astype(BF)
        return carry

    lax.fori_loop(0, 4, spread_t, 0)

    m2 = lax.broadcasted_iota(jnp.int32, (C, 512), 1)
    ch2 = lax.broadcasted_iota(jnp.int32, (C, 512), 0)
    in2 = jnp.bitwise_and(m2, 15)
    pick2 = jnp.logical_and(in2 < 12, ch2 == 12 * lax.shift_right_logical(m2, 4) + in2)
    sel2 = jnp.where(pick2, 1.0, 0.0).astype(BF)

    for o in offsets:
        cc1[o].arrived()
        cc2[o].arrived()
    for j in range(4):
        w_in[j] = nn(sel2, gath[:, 16 * j : 16 * j + 16, :].reshape(512, C)).astype(BF)

    for j in range(4):
        wo = gath[8 * j : 8 * j + 8, 64:112, :].reshape(C, C)

        def forward(i, carry, j=j, wo=wo):
            cells = pl.ds(pl.multiple_of(i * 256, 256), 256)
            h = nn(normed[cells, :], w_in[j])
            value, grad = gelu_pair(h)
            value = value.astype(BF)
            act[cells, :] = value
            slope[j, cells, :] = grad
            mix = nn(value, wo)
            if j:
                mixed[cells, :] += mix
            else:
                mixed[cells, :] = mix
            return carry

        lax.fori_loop(0, 4, forward, 0)
        part = tn(act[...], gm[...]).astype(BF)
        for u in range(8):
            for i in range(3):
                ro[u % 2, i, 4 * j + u // 2] = part[48 * u + 16 * i : 48 * u + 16 * i + 16]

    has_out = y < 3

    class Reduction:
        def __init__(self, whole, cp, yp, xp, xr, zp, zr, f, uneven):
            self.__dict__.update(locals())
            pieces = 3 if uneven else 4
            on = has_out if uneven else None
            keep = pl.ds(0, pieces)
            self.on = on
            self.c = [Copy(sems, whole.at[1 - core, keep], cp.at[keep], other_core)]
            self.y, self.g = [], []
            for k in range(1, NY):
                yy, ys = ring(y, k, NY), ring(y, -k, NY)
                self.y.append(
                    Copy(
                        sems, cp.at[yy], yp.at[k - 1], ydev(k),
                        send_if=yy < 3 if uneven else None, recv_if=on,
                    )
                )
                self.g.append(
                    Copy(
                        sems, f.at[y], f.at[y], ydev(k), land=f.at[ys],
                        send_if=on, recv_if=ys < 3 if uneven else None,
                    )
                )
            self.x = []
            for k in range(1, NX):
                xx = ring(x, k, NX)
                self.x.append(
                    Copy(
                        sems, xp.at[pl.ds(lax.rem(xx, 2) * NZ, NZ)], xr.at[k - 1], xdev(k),
                        send_if=on, recv_if=on,
                    )
                )
            self.z = [
                Copy(sems, zp.at[ring(z, k, NZ)], zr.at[k - 1], zdev(k), send_if=on, recv_if=on)
                for k in range(1, NZ)
            ]
            self.pieces = pieces

        def when(self, fn):
            if self.on is None:
                fn()
            else:
                pl.when(self.on)(fn)

        def go_core(self):
            begin(self.c)

        def go_y(self):
            self.c[0].arrived()

            def add(i, carry):
                for n in range(self.pieces):
                    a = self.whole[core, n, i].astype(F32) + self.cp[n, i].astype(F32)
                    self.cp[n, i] = a.astype(BF)
                return carry

            lax.fori_loop(0, 16, add, 0)
            begin(self.y)

        def go_x(self):
            for c in self.y:
                c.arrived()

            def fn():
                def add(i, carry):
                    a = self.cp[y, i].astype(F32)
                    for n in range(3):
                        a = a + self.yp[n, i].astype(F32)
                    self.xp[i] = a.astype(BF)
                    return carry

                lax.fori_loop(0, 16, add, 0)

            self.when(fn)
            begin(self.x)

        def go_z(self):
            for c in self.x:
                c.arrived()

            def fn():
                def add(i, carry):
                    a = self.xp[xlo * NZ + i].astype(F32)
                    for n in range(3):
                        a = a + self.xr[n, i].astype(F32)
                    self.zp[i] = a.astype(BF)
                    return carry

                lax.fori_loop(0, NZ, add, 0)

            self.when(fn)
            begin(self.z)

        def go_gather(self):
            for c in self.z:
                c.arrived()

            def fn():
                a = self.zp[z].astype(F32)
                for n in range(NZ - 1):
                    a = a + self.zr[n].astype(F32)
                self.f[y] = a * NORM

            self.when(fn)
            begin(self.g)

        def finish(self):
            for c in self.g:
                c.arrived()

    NORM = 1.0 / math.sqrt(256 * 1024)
    out_sum = Reduction(ro, cpo, ypo, xpo, xro, zpo, zro, fo, True)
    in_sum = Reduction(ri, cpi, ypi, xpi, xri, zpi, zri, fi, False)
    out_sum.go_core()

    for j in range(4):
        wo = gath[8 * j : 8 * j + 8, 64:112, :].reshape(C, C)

        def backward(i, carry, j=j, wo=wo):
            cells = pl.ds(pl.multiple_of(i * 256, 256), 256)
            ga = nt(gm[cells, :], wo)
            g = (ga * slope[j, cells, :]).astype(BF)
            gh[cells, :] = g
            back = nt(g, w_in[j])
            if j:
                gn[cells, :] += back
            else:
                gn[cells, :] = back
            return carry

        lax.fori_loop(0, 4, backward, 0)
        part = nn(npt[...], gh[...]).astype(BF)
        ri[:, j] = part.reshape(2, 16, 16, C)
        if j == 1:
            out_sum.go_y()
    in_sum.go_core()

    def norm_back(r, carry):
        cells = pl.ds(pl.multiple_of(r * COLS, COLS), COLS)
        unit = conv[r]
        g = gn[cells, :] * gain
        sp = spread_b[r]
        sp = jnp.concatenate([sp, sp, sp], axis=1)
        first = jnp.mean(g, axis=-1, keepdims=True)
        second = jnp.mean(g * unit, axis=-1, keepdims=True)
        gc = sp * (g - first - unit * second)
        gn[cells, :] = gc
        ghalf[r] = gc.astype(BF)
        return carry

    lax.fori_loop(0, ROWS, norm_back, 0)
    halo2 = halo_copies(ghalf, 1)
    begin(halo2)
    in_sum.go_y()
    out_sum.go_x()

    for r in range(ROWS):
        row_scale = scale * flags[r]
        cells = pl.ds(COLS * r, COLS)
        new_ref[r] = (x_ref[r].astype(F32) + row_scale * mixed[cells, :]).astype(BF)

    for t in range(TAPS * TAPS, 64):
        kp[t // 8, t % 8 : t % 8 + 1, :] = jnp.zeros((1, C), F32)

    def tap_sums(l, carry):
        for b in range(TAPS):
            def body(cg, acc, b=b):
                c0 = pl.multiple_of(cg * 8, 8)
                rows = [ext[l, row, pl.ds(c0 + 5 + b, 8), :] for row in range(ROWS + 2 * REACH)]
                acc = list(acc)
                for r in range(ROWS):
                    g = gn[pl.ds(c0 + COLS * r, 8), lanes(l)]
                    for a in range(TAPS):
                        acc[a] = acc[a] + g * rows[r + a]
                return tuple(acc)

            acc = lax.fori_loop(0, 16, body, (jnp.zeros((8, 128), F32),) * TAPS)
            for a in range(TAPS):
                t = a * TAPS + b
                kp[t // 8, t % 8 : t % 8 + 1, lanes(l)] = jnp.sum(acc[a], axis=0, keepdims=True)
        return carry

    lax.fori_loop(0, 1, tap_sums, 0)
    out_sum.go_z()
    lax.fori_loop(1, 2, tap_sums, 0)
    lax.fori_loop(2, 3, tap_sums, 0)

    kz_c = [Copy(sems, kp.at[ring(z, k, NZ)], kz.at[k - 1], zdev(k)) for k in range(1, NZ)]
    kc_c = [Copy(sems, kcs, kc, other_core)]
    kx_c = [Copy(sems, kxs, kx.at[k - 1], xdev(k)) for k in range(1, NX)]
    ky_c = [Copy(sems, kys, ky.at[k - 1], ydev(k)) for k in range(1, NY)]
    kf_c = [
        Copy(sems, kf.at[z], kf.at[z], zdev(k), land=kf.at[ring(z, -k, NZ)]) for k in range(1, NZ)
    ]
    begin(kz_c)
    for c in halo2:
        c.arrived()
    extend(ghalf, 1, ext2)

    def arrive_all(copies):
        for c in copies:
            c.arrived()

    def emit_back(r, cs, ls, v):
        gs_part[r, cs, ls] = v

    gs_part = conv
    arrive_all(kz_c)
    total = kp[z]
    for n in range(NZ - 1):
        total = total + kz[n]
    kcs[...] = total
    begin(kc_c)
    in_sum.go_x()
    out_sum.go_gather()
    stencil(ext2, True, emit_back, 0, 16)
    arrive_all(kc_c)
    kxs[...] = kcs[...] + kc[...]
    begin(kx_c)
    in_sum.go_z()
    stencil(ext2, True, emit_back, 16, 32)
    arrive_all(kx_c)
    kys[...] = kxs[...] + kx[0] + kx[1] + kx[2]
    begin(ky_c)
    in_sum.go_gather()
    stencil(ext2, True, emit_back, 32, 48)
    arrive_all(ky_c)
    kf[z] = (kys[...] + ky[0] + ky[1] + ky[2]) * NORM
    begin(kf_c)

    def finish_row(r, carry):
        gs_ref[r] = (cot_ref[r].astype(F32) + gs_part[r]).astype(BF)
        return carry

    lax.fori_loop(0, ROWS, finish_row, 0)
    out_sum.finish()
    for i in range(3):
        gwo_ref[16 * i : 16 * i + 16, :] = fo[i]
    in_sum.finish()
    for j in range(4):
        gwi_ref[:, C * j : C * (j + 1)] = fi[j, 0:12, :]
    arrive_all(kf_c)
    for n in range(6):
        gk_ref[8 * n : 8 * n + 8, :] = kf[n]
    gk_ref[48:49, :] = kf[6, 0:1, :]
    for c in started:
        c.left()


def per_device(
    ocean_state, kernel, norm_gain, weight_in, weight_out, layer_scale, cotangent, tile_list, ocean_count
):
    vmem = pl.BlockSpec(memory_space=pltpu.VMEM)
    smem = pl.BlockSpec(memory_space=pltpu.SMEM)
    V = pltpu.VMEM
    scratch = [
        V((2, 2, REACH, COLS, C), BF),
        V((2, 2, ROWS, 16, C), BF),
        V((2, 4, REACH, 16, C), BF),
        V((3, 14, 144, 128), F32),
        V((3, 14, 144, 128), F32),
        V((3, 49, 8, 128), F32),
        V((ROWS, COLS, C), F32),
        V((ROWS, COLS, 128), F32),
        V((ROWS * COLS, C), BF),
        V((512, ROWS * COLS), BF),
        V((ROWS * COLS, C), BF),
        V((ROWS, COLS, C), BF),
        V((32, 112, C), BF),
        V((4, C, C), BF),
        V((512, C), BF),
        V((ROWS * COLS, C), BF),
        V((4, ROWS * COLS, C), F32),
        V((ROWS * COLS, C), BF),
        V((ROWS * COLS, C), F32),
        V((ROWS * COLS, C), F32),
        V((2, 4, 16, 16, C), BF),
        V((2, 4, 16, 16, C), BF),
        V((4, 16, 16, C), BF),
        V((4, 16, 16, C), BF),
        V((3, 16, 16, C), BF),
        V((3, 16, 16, C), BF),
        V((16, 16, C), BF),
        V((16, 16, C), BF),
        V((3, NZ, 16, C), BF),
        V((3, NZ, 16, C), BF),
        V((NZ, 16, C), BF),
        V((NZ, 16, C), BF),
        V((NZ - 1, 16, C), BF),
        V((NZ - 1, 16, C), BF),
        V((4, 16, C), F32),
        V((4, 16, C), F32),
        V((NZ, 8, C), F32),
        V((NZ - 1, 8, C), F32),
        V((8, C), F32),
        V((3, 8, C), F32),
        V((3, 8, C), F32),
        V((8, C), F32),
        V((8, C), F32),
        V((8, C), F32),
        V((NZ, 8, C), F32),
        pltpu.SemaphoreType.DMA((N_SEM,)),
        pltpu.SemaphoreType.DMA((N_SEM,)),
    ]
    return pl.pallas_call(
        kernel_body,
        out_shape=(
            jax.ShapeDtypeStruct((ROWS, COLS, C), BF),
            jax.ShapeDtypeStruct((ROWS, COLS, C), BF),
            jax.ShapeDtypeStruct((12, FF), F32),
            jax.ShapeDtypeStruct((48, C), F32),
            jax.ShapeDtypeStruct((TAPS * TAPS, C), F32),
        ),
        in_specs=[smem, smem] + [vmem] * 7,
        out_specs=(vmem,) * 5,
        scratch_shapes=scratch,
        compiler_params=pltpu.CompilerParams(
            collective_id=0, has_side_effects=True, vmem_limit_bytes=60 * 2**20
        ),
        cost_estimate=pl.CostEstimate(
            flops=8 * 10**9, bytes_accessed=4 * 10**6, transcendentals=4 * 10**6
        ),
        name="block",
    )(
        tile_list, ocean_count, ocean_state, kernel, norm_gain.reshape(1, C), weight_in, weight_out,
        layer_scale.reshape(1, C), cotangent,
    )


def solution(mesh):
    return jax.shard_map(
        per_device,
        mesh=mesh,
        in_specs=(
            P("lat", "lon", None),
            P(),
            P(),
            P("lat", None),
            P("lat", None),
            P(),
            P("lat", "lon", None),
            P("lat", "lon", None),
            P("lat", "lon"),
        ),
        out_specs=(
            P("lat", "lon", None),
            P("lat", "lon", None),
            P("lat", None),
            P("lat", None),
            P(),
        ),
        check_vma=False,
    )
```

time: 482 us -> 117 us (0.24)
  waiting for transfers between devices: 330 us -> 0 us
  Pallas kernels: 0 us -> 108 us
  other arithmetic: 69.8 us -> 0 us
  starting transfers between devices: 22.3 us -> 0 us
  matrix products: 21.3 us -> 0 us
  between operations: 15.8 us -> 1.31 us
  local copies, waits for them, and re-layouts: 19.3 us -> 7.42 us
    psum x1 -> x0, waiting for transfers between devices: 252 us -> none  [per_device(): lax.psum((part_in, part_out, part_kernel), ('lat', 'lon'))]
    pallas_call x0 -> x1, Pallas kernels: none -> 108 us  [per_device(): pl.pallas_call(kernel_body, out_shape=(jax.ShapeDtypeStruct((ROWS, COLS,...]
    all_gather x2 -> x0, waiting for transfers between devices: 75.5 us -> none  [the longest x1 56.4 us: per_device(): lax.all_gather(weight_out, 'lat', axis=0, tiled=True)]
    reduce_sum x10 -> x0, other arithmetic: 41.3 us -> none  [the longest x1 20.6 us: pointwise(): centre = conv_rows - jnp.mean(conv_rows, axis=-1, keepdims=True)]
    ppermute x8 -> x0, starting transfers between devices: 22.2 us -> none  [the longest x4 16.6 us: padded_2(): after = lax.ppermute(leading, axis, down)]
    dot_general x6 -> x0, matrix products: 21.3 us -> none  [the longest x2 7.45 us: contract_cols(): lax.dot_general(left, right, (((1,), (1,)), ((), ())), preferred_element_...]
    convert_element_type x6 -> x0, other arithmetic: 21.2 us -> none  [the longest x1 17 us: per_device(): (cotangent.astype(jnp.float32) + spread_back).astype(jnp.bfloat16)]
    slice x6 -> x0, local copies, waits for them, and re-layouts: 7.94 us -> none  [the longest x3 5.39 us: stencil(): kernel[row_tap * TAPS + col_tap] * window.astype(jnp.float32)]
  transfers between devices with their start and end apart: 11 -> 0, of which waited for: 5 -> 0; matrix products, arithmetic and copies ran while one was open for 18% -> 0% of each run, Pallas kernels for 0% -> 0%
where the time goes in v1:
time: 117 us
  Pallas kernels  108 us (92%)
  local copies, waits for them, and re-layouts  7.42 us (6%)
  between operations  1.31 us (1%)
    pallas_call x1, Pallas kernels, per_device(): pl.pallas_call(kernel_body, out_shape=(jax.ShapeDtypeStruct((ROWS, COLS,...  108 us
    unnamed x15, local copies, waits for them, and re-layouts  5.61 us

profile of v1, /device:TPU:32, one launch (start us, length us, event | category | flops | bytes accessed | tf_op | source)
XLA Modules:
  0.0 116.8 jit_solution(15678606439840416694)
XLA Ops:
  1.3 0.0 copy-start.4
  1.3 1.3 %reshape.16.gain_ref = f32[1,384]{1,0:T(1,128)} reshape(f32[384]{0:T(512)} %param.11) | data formatting | bytes 3072 | tf_op jit(solution)/shard_map/reshape | solution.py:676
  2.5 0.0 copy-done.4
  2.5 0.6 reshape.17.scale_ref
  3.1 108.0 %block.1 = (bf16[8,128,384]{2,1,0:T(8,128)(2,1)}, bf16[8,128,384]{2,1,0:T(8,128)(2,1)}, f32[12,1536]{1,0:T(8,128)}, f32[48,384]{1,0:T(8,128)}, f32[49,384]{1,0:T(8,128)}) custom-call(s32[1,1,6]{2,1,0:T(1,128)} %tile_ref.1, s32[1,1]{1,0:T(1,128)S(6)} %copy.19.count_ref, bf16[8,128,384]{2,1,0:T(8,128)(2,1)} %x_ref.1, f32[49,384]{1,0:T(8,128)} %k_ref.1, ...), custom_call_target="tpu_custom_call" | custom-call | flops 8000000000 | bytes 4000000 | tf_op jit(solution)/shard_map/block/pallas_call | solution.py:656
  111.1 0.0 copy-start
  111.1 2.2 %copy.20 = bf16[8,128,384]{2,1,0:T(8,128)(2,1)} copy(bf16[8,128,384]{2,1,0:T(8,128)(2,1)} %get-tuple-element.10) | data formatting | bytes 1572864
  113.3 0.0 copy-done
  113.3 0.0 copy-start.1
  113.3 0.9 copy.21
  114.2 0.1 copy-done.1
  114.3 0.0 copy-start.3
  114.3 0.6 copy.22
  114.9 0.3 copy-done.3
  115.2 0.0 copy-start.2
  115.2 0.6 copy.23
  115.8 0.3 copy-done.2
  116.1 0.6 copy.24
Async XLA Ops:
  1.3 1.3 %copy-start.4 = (f32[384]{0:T(512)S(1)}, f32[384]{0:T(512)}, u32[]{:S(2)}) copy-start(f32[384]{0:T(512)} %param.14) | copy-start | bytes 4612
  111.1 2.2 %copy-start = (bf16[8,128,384]{2,1,0:T(8,128)(2,1)S(1)}, bf16[8,128,384]{2,1,0:T(8,128)(2,1)}, u32[]{:S(2)}) copy-start(bf16[8,128,384]{2,1,0:T(8,128)(2,1)} %get-tuple-element.11) | copy-start | bytes 2359300
  113.3 1.0 copy-start.1
  114.3 0.9 copy-start.3
  115.2 0.9 copy-start.2

commit v2 on v1

v2 whole, which is shorter than its diff:
```python
import functools
import math

import jax
import jax.numpy as jnp
from jax import lax
from jax.experimental import pallas as pl
from jax.experimental.pallas import tpu as pltpu
from jax.sharding import PartitionSpec as P

TAPS = 7
REACH = 3
ROWS = 8
COLS = 128
C = 384
FF = 1536
NZ = 8
NY = 4
NX = 4
EPS = 1e-06
ROOT_HALF = 0.7071067811865476
INV_ROOT_TWO_PI = 0.3989422804014327
BF = jnp.bfloat16
F32 = jnp.float32
MESH = pl.DeviceIdType.MESH
N_SEM = 192
HALVES = 2
HALF = FF // HALVES


def gelu_pair(h):
    cdf = 0.5 * (1.0 + lax.erf(h * ROOT_HALF))
    return h * cdf, cdf + h * (INV_ROOT_TWO_PI * jnp.exp(-0.5 * h * h))


def nt(left, right):
    return lax.dot_general(left, right, (((1,), (1,)), ((), ())), preferred_element_type=F32)


def tn(left, right):
    return lax.dot_general(left, right, (((0,), (0,)), ((), ())), preferred_element_type=F32)


def nn(left, right):
    return jnp.dot(left, right, preferred_element_type=F32)


class Copy:
    def __init__(self, sems, src, dst, dev, land=None, send_if=None, recv_if=None):
        send, recv, counter = sems
        self.slot = counter[0]
        counter[0] += 1
        self.send_sem, self.recv_sem = send.at[self.slot], recv.at[self.slot]
        self.src, self.dst, self.dev = src, dst, dev
        self.land = dst if land is None else land
        self.send_if, self.recv_if = send_if, recv_if

    def _make(self, dst):
        return pltpu.make_async_remote_copy(
            src_ref=self.src,
            dst_ref=dst,
            send_sem=self.send_sem,
            recv_sem=self.recv_sem,
            device_id=self.dev,
            device_id_type=MESH,
        )

    def start(self):
        if self.send_if is None:
            self._make(self.dst).start()
        else:
            pl.when(self.send_if)(lambda: self._make(self.dst).start())

    def arrived(self):
        if self.recv_if is None:
            self._make(self.land).wait_recv()
        else:
            pl.when(self.recv_if)(lambda: self._make(self.land).wait_recv())

    def left(self):
        if self.send_if is None:
            self._make(self.dst).wait_send()
        else:
            pl.when(self.send_if)(lambda: self._make(self.dst).wait_send())


def kernel_body(
    tile_ref, count_ref, x_ref, k_ref, gain_ref, win_ref, wout_ref, scale_ref, cot_ref,
    new_ref, gs_ref, gwi_ref, gwo_ref, gk_ref,
    hrow, hcol, hcor, ext, ext2, k8, conv, spread_b, normed, npt, gm, ghalf,
    pack, gin, gout, unpack, w_in, sel, act, slope, gh, mixed, gn,
    ro, ri, cpo, cpi, ypo, ypi, xpo, xpi, xro, xri, zpo, zpi, zro, zri, fo, fi,
    kp, kz, kc, kx, ky, kcs, kxs, kys, kf,
    send, recv,
):
    lat, lon = lax.axis_index("lat"), lax.axis_index("lon")
    core, z, xlo = lax.rem(lat, 2), lax.rem(lat // 2, NZ), lat // (2 * NZ)
    y, xhi = lax.rem(lon, NY), lon // NY
    x = xhi * 2 + xlo
    q = xlo * NZ + z
    sems = (send, recv, [0])

    def at(xx, zz, cc, yy):
        return ((lax.rem(xx, 2) * NZ + zz) * 2 + cc, (xx // 2) * NY + yy)

    def ring(v, k, n):
        return lax.rem(v + k + n, n)

    def zdev(k):
        return at(x, ring(z, k, NZ), core, y)

    def xdev(k):
        return at(ring(x, k, NX), z, core, y)

    def ydev(k):
        return at(x, z, core, ring(y, k, NY))

    other_core = at(x, z, 1 - core, y)

    def around(dr, dc):
        return (ring(lat, dr, 32), ring(lon, dc, 8))

    barrier = pltpu.get_barrier_semaphore()
    partners = [around(dr, dc) for dr in (-1, 0, 1) for dc in (-1, 0, 1) if dr or dc]
    partners += [zdev(k) for k in range(1, NZ)]
    partners += [xdev(k) for k in range(1, NX)]
    partners += [ydev(k) for k in range(1, NY)]
    partners += [other_core]
    for dev in partners:
        pl.semaphore_signal(barrier, inc=1, device_id=dev, device_id_type=MESH)

    for b in range(3):
        pack[b, 0:12, :] = win_ref[:, C * b : C * (b + 1)].astype(F32)
        pack[b, 12:16, :] = win_ref[4 * b : 4 * b + 4, 3 * C : 4 * C].astype(F32)
        gin[lat, b] = pack[b].astype(BF)
    gout[lat] = wout_ref[...]
    pl.semaphore_wait(barrier, len(partners))

    started = []

    def begin(copies):
        for c in copies:
            c.start()
            started.append(c)

    def halo_copies(src, n):
        top, bottom = pl.ds(0, REACH), pl.ds(ROWS - REACH, REACH)
        first, last, every = pl.ds(0, 16), pl.ds(COLS - 16, 16), pl.ds(0, ROWS)
        out = [
            Copy(sems, src.at[bottom], hrow.at[n, 0], around(1, 0)),
            Copy(sems, src.at[top], hrow.at[n, 1], around(-1, 0)),
            Copy(sems, src.at[every, last], hcol.at[n, 0], around(0, 1)),
            Copy(sems, src.at[every, first], hcol.at[n, 1], around(0, -1)),
            Copy(sems, src.at[bottom, last], hcor.at[n, 0], around(1, 1)),
            Copy(sems, src.at[bottom, first], hcor.at[n, 1], around(1, -1)),
            Copy(sems, src.at[top, last], hcor.at[n, 2], around(-1, 1)),
            Copy(sems, src.at[top, first], hcor.at[n, 3], around(-1, -1)),
        ]
        return out

    halo1 = halo_copies(x_ref, 0)
    begin(halo1)

    def shard(xl, zz, cc):
        return (xl * NZ + zz) * 2 + cc

    order = [1, 7, 2, 6, 3, 5, 4]
    olo = 1 - xlo

    class Gather:
        def __init__(self, buf):
            self.z, self.x, self.c1, self.c2 = {}, {}, {}, {}
            mine = buf.at[lat]
            for i, k in enumerate([0] + order):
                zz = ring(z, -k, NZ)
                s, so = shard(xlo, zz, core), shard(olo, zz, core)
                far, faro = shard(xlo, zz, 1 - core), shard(olo, zz, 1 - core)
                if k:
                    self.z[k] = Copy(sems, mine, mine, zdev(k), land=buf.at[s])
                self.x[k] = Copy(
                    sems, buf.at[s], buf.at[s], xdev(1 if i % 2 == 0 else -1), land=buf.at[so]
                )
                self.c1[k] = Copy(sems, buf.at[s], buf.at[s], other_core, land=buf.at[far])
                self.c2[k] = Copy(sems, buf.at[so], buf.at[so], other_core, land=buf.at[faro])

        def launch(self):
            begin([self.z[k] for k in order] + [self.x[0], self.c1[0]])

        def onward(self, *ks):
            for k in ks:
                self.z[k].arrived()
                begin([self.x[k], self.c1[k]])

        def across(self, *ks):
            for k in ks:
                self.x[k].arrived()
                begin([self.c2[k]])

        def done(self):
            for k in [0] + order:
                self.c1[k].arrived()
                self.c2[k].arrived()

    gather_in, gather_out = Gather(gin), Gather(gout)
    gather_in.launch()

    flags = []
    for r in range(ROWS):
        hit = jnp.int32(0)
        for s in range(6):
            match = jnp.logical_and(tile_ref[0, 0, s] == r, s < count_ref[0, 0])
            hit = hit + jnp.where(match, 1, 0)
        flags.append(hit.astype(F32))
    for l in range(3):
        for t in range(TAPS * TAPS):
            k8[l, t] = jnp.broadcast_to(k_ref[t : t + 1, 128 * l : 128 * (l + 1)], (8, 128))
    gain = gain_ref[...].reshape(1, C)
    scale = scale_ref[...].reshape(1, C)
    for r in range(ROWS):
        row_scale = scale * flags[r]
        gm[pl.ds(COLS * r, COLS), :] = (row_scale * cot_ref[r].astype(F32)).astype(BF)

    def lanes(l):
        return pl.ds(pl.multiple_of(l * 128, 128), 128)

    def put_row(dst, row, mid, on):
        for l in range(3):
            m = mid[:, 128 * l : 128 * (l + 1)].astype(F32)
            dst[l, row, 8 : 8 + COLS, :] = m if on is None else m * on

    def put_sides(dst, row, left, right, on):
        for l in range(3):
            sl = slice(128 * l, 128 * (l + 1))
            a, b = left[:, sl].astype(F32), right[:, sl].astype(F32)
            if on is not None:
                a, b = a * on, b * on
            dst[l, row, 0:8, :] = a[8:16]
            dst[l, row, 8 + COLS : 16 + COLS, :] = b[0:8]

    def extend_own(src, dst):
        def middle(r, carry):
            put_row(dst, REACH + r, src[r], None)
            return carry

        lax.fori_loop(0, ROWS, middle, 0)

    def extend_rim(n, dst):
        up_on = jnp.where(lat > 0, 1.0, 0.0).astype(F32)
        down_on = jnp.where(lat < 31, 1.0, 0.0).astype(F32)

        def middle(r, carry):
            put_sides(dst, REACH + r, hcol[n, 0, r], hcol[n, 1, r], None)
            return carry

        def outer(r, carry):
            put_row(dst, r, hrow[n, 0, r], up_on)
            put_sides(dst, r, hcor[n, 0, r], hcor[n, 1, r], up_on)
            put_row(dst, REACH + ROWS + r, hrow[n, 1, r], down_on)
            put_sides(dst, REACH + ROWS + r, hcor[n, 2, r], hcor[n, 3, r], down_on)
            return carry

        lax.fori_loop(0, ROWS, middle, 0)
        lax.fori_loop(0, REACH, outer, 0)

    own_rows = tuple(range(REACH, REACH + ROWS))
    rim_rows = tuple(range(REACH)) + tuple(range(REACH + ROWS, 2 * REACH + ROWS))

    def tile_sums(src, flipped, l, c0, rows_in, acc):
        for b in range(TAPS):
            rows = {row: src[l, row, pl.ds(c0 + 5 + b, 8), :] for row in rows_in}
            for a in range(TAPS):
                t = a * TAPS + b
                tap = k8[l, TAPS * TAPS - 1 - t if flipped else t]
                for r in range(ROWS):
                    if r + a in rows:
                        term = tap * rows[r + a]
                        acc[r] = term if acc[r] is None else acc[r] + term
        return acc

    def stencil(src, flipped, out, first, last):
        def body(i, carry):
            l, c0 = i // 16, pl.multiple_of(lax.rem(i, 16) * 8, 8)
            acc = tile_sums(src, flipped, l, c0, own_rows + rim_rows, [None] * ROWS)
            for r in range(ROWS):
                out[r, pl.ds(c0, 8), lanes(l)] = acc[r]
            return carry

        lax.fori_loop(first, last, body, 0)

    def stencil_own(src, out, first, last):
        def body(i, carry):
            l, c0 = i // 14, pl.multiple_of(lax.rem(i, 14) * 8 + 8, 8)
            acc = tile_sums(src, False, l, c0, own_rows, [None] * ROWS)
            for r in range(ROWS):
                out[r, pl.ds(c0, 8), lanes(l)] = acc[r]
            return carry

        lax.fori_loop(first, last, body, 0)

    def stencil_rim(src, out):
        touched = (0, 1, 2, 5, 6, 7)

        def body(i, carry):
            l, c0 = i // 14, pl.multiple_of(lax.rem(i, 14) * 8 + 8, 8)
            acc = [out[r, pl.ds(c0, 8), lanes(l)] if r in touched else None for r in range(ROWS)]
            acc = tile_sums(src, False, l, c0, rim_rows, acc)
            for r in touched:
                out[r, pl.ds(c0, 8), lanes(l)] = acc[r]
            return carry

        def sides(i, carry):
            l, c0 = i // 2, pl.multiple_of(lax.rem(i, 2) * 120, 8)
            acc = tile_sums(src, False, l, c0, own_rows + rim_rows, [None] * ROWS)
            for r in range(ROWS):
                out[r, pl.ds(c0, 8), lanes(l)] = acc[r]
            return carry

        lax.fori_loop(0, 42, body, 0)
        lax.fori_loop(0, 6, sides, 0)

    extend_own(x_ref, ext)
    stencil_own(ext, conv, 0, 42)
    gather_in.onward(1, 7)
    gather_out.launch()
    for c in halo1:
        c.arrived()
    extend_rim(0, ext)
    gather_in.onward(2, 6)
    gather_in.across(0)
    stencil_rim(ext, conv)
    gather_in.onward(3, 5)
    gather_in.across(1, 7)

    def norm_row(r, carry):
        v = conv[r]
        centre = v - jnp.mean(v, axis=-1, keepdims=True)
        sp = lax.rsqrt(jnp.mean(centre * centre, axis=-1, keepdims=True) + EPS)
        unit = centre * sp
        conv[r] = unit
        spread_b[r] = jnp.broadcast_to(sp, (COLS, 128))
        normed[pl.ds(pl.multiple_of(r * COLS, COLS), COLS), :] = (unit * gain).astype(BF)
        return carry

    lax.fori_loop(0, ROWS, norm_row, 0)
    gather_in.onward(4)
    gather_in.across(2, 6)
    gather_out.onward(1, 7)

    m = lax.broadcasted_iota(jnp.int32, (C, C), 0)
    ch = lax.broadcasted_iota(jnp.int32, (C, C), 1)
    half = jnp.where(m >= 192, 1, 0)
    u = m - 192 * half
    inside = u - 12 * lax.shift_right_logical(u * 5462, 16)
    sel[...] = jnp.where(ch == 2 * u - inside + 12 * half, 1.0, 0.0).astype(BF)
    npt[...] = nt(sel[...], normed[...]).astype(BF)

    m2 = lax.broadcasted_iota(jnp.int32, (C, 512), 1)
    ch2 = lax.broadcasted_iota(jnp.int32, (C, 512), 0)
    in2 = jnp.bitwise_and(m2, 15)
    at2 = 12 * lax.shift_right_logical(m2, 4) + in2
    for b in range(3):
        top = jnp.logical_and(in2 < 12, ch2 == at2)
        low = jnp.logical_and(in2 >= 12, ch2 == at2 + 4 * b - 12)
        unpack[0] = jnp.where(top, 1.0, 0.0).astype(BF)
        unpack[1 + b] = jnp.where(low, 1.0, 0.0).astype(BF)
    gather_in.across(3, 5, 4)
    gather_out.onward(2, 6)
    gather_out.across(0, 1, 7)
    gather_in.done()
    rest = None
    for b in range(3):
        g = gin[:, b].reshape(512, C)
        w_in[b // 2, :, C * (b % 2) : C * (b % 2 + 1)] = nn(unpack[0], g).astype(BF)
        low = nn(unpack[1 + b], g)
        rest = low if b == 0 else rest + low
    w_in[1, :, C:] = rest.astype(BF)

    for j in range(HALVES):
        h = nn(normed[...], w_in[j])
        value, grad = gelu_pair(h)
        act[j] = value.astype(BF)
        slope[j] = grad
        if j == 0:
            gather_out.onward(3, 5, 4)
            gather_out.across(2, 6)
    gather_out.across(3, 5, 4)
    gather_out.done()
    for j in range(HALVES):
        part = tn(act[j], gm[...]).astype(BF)
        for u in range(16):
            q_to = 8 * j + u // 2
            for i in range(3):
                ro[u % 2, i, 16 * q_to : 16 * q_to + 16] = part[48 * u + 16 * i : 48 * u + 16 * i + 16]

    has_out = y < 3

    class Reduction:
        def __init__(self, whole, cp, yp, xp, xr, zp, zr, f, uneven):
            self.__dict__.update(locals())
            on = has_out if uneven else None
            self.on = on
            self.pieces = 3 if uneven else 4
            self.rows = whole.shape[2]
            self.part = self.rows // 2
            self.c = [Copy(sems, whole.at[1 - core], cp, other_core)]
            self.y, self.g = [], []
            for k in range(1, NY):
                yy, ys = ring(y, k, NY), ring(y, -k, NY)
                last = self.pieces - 1
                self.y.append(
                    Copy(
                        sems, cp.at[jnp.minimum(yy, last)], yp.at[k - 1], ydev(k),
                        send_if=yy < 3 if uneven else None, recv_if=on,
                    )
                )
                self.g.append(
                    Copy(
                        sems, f.at[jnp.minimum(y, last)], f.at[jnp.minimum(y, last)], ydev(k),
                        land=f.at[jnp.minimum(ys, last)],
                        send_if=on, recv_if=ys < 3 if uneven else None,
                    )
                )
            self.x = []
            for k in range(1, NX):
                xx = ring(x, k, NX)
                self.x.append(
                    Copy(
                        sems, xp.at[self.side(lax.rem(xx, 2))], xr.at[k - 1], xdev(k),
                        send_if=on, recv_if=on,
                    )
                )
            self.z = [
                Copy(sems, zp.at[ring(z, k, NZ)], zr.at[k - 1], zdev(k), send_if=on, recv_if=on)
                for k in range(1, NZ)
            ]

        def side(self, lo):
            return pl.ds(pl.multiple_of(lo * self.part, 16), self.part)

        def when(self, fn):
            if self.on is None:
                fn()
            else:
                pl.when(self.on)(fn)

        def go_core(self):
            begin(self.c)

        def go_y(self):
            self.c[0].arrived()

            def add(i, carry):
                rows = pl.ds(pl.multiple_of(i * 64, 16), 64)
                for n in range(self.pieces):
                    a = self.whole[core, n, rows].astype(F32) + self.cp[n, rows].astype(F32)
                    self.cp[n, rows] = a.astype(BF)
                return carry

            lax.fori_loop(0, self.rows // 64, add, 0)
            begin(self.y)

        def go_x(self):
            for c in self.y:
                c.arrived()

            def fn():
                own = jnp.minimum(y, self.pieces - 1)

                def add(i, carry):
                    rows = pl.ds(pl.multiple_of(i * 64, 16), 64)
                    a = self.cp[own, rows].astype(F32)
                    for n in range(3):
                        a = a + self.yp[n, rows].astype(F32)
                    self.xp[rows] = a.astype(BF)
                    return carry

                lax.fori_loop(0, self.rows // 64, add, 0)

            self.when(fn)
            begin(self.x)

        def go_z(self):
            for c in self.x:
                c.arrived()

            def fn():
                a = self.xp[self.side(xlo)].astype(F32)
                for n in range(3):
                    a = a + self.xr[n].astype(F32)
                a = a.astype(BF)
                if self.part != NZ * 16:
                    to = lax.broadcasted_iota(jnp.int32, (NZ * 16, self.part), 0)
                    fr = lax.broadcasted_iota(jnp.int32, (NZ * 16, self.part), 1)
                    slot = jnp.bitwise_and(to, 15)
                    pick = jnp.logical_and(
                        slot < 12, fr == 12 * lax.shift_right_logical(to, 4) + slot
                    )
                    a = nn(jnp.where(pick, 1.0, 0.0).astype(BF), a).astype(BF)
                self.zp[...] = a.reshape(NZ, 16, C)

            self.when(fn)
            begin(self.z)

        def go_gather(self):
            for c in self.z:
                c.arrived()

            def fn():
                a = self.zp[z].astype(F32)
                for n in range(NZ - 1):
                    a = a + self.zr[n].astype(F32)
                self.f[jnp.minimum(y, self.pieces - 1)] = a * NORM

            self.when(fn)
            begin(self.g)

        def finish(self):
            for c in self.g:
                c.arrived()

    NORM = 1.0 / math.sqrt(256 * 1024)
    out_sum = Reduction(ro, cpo, ypo, xpo, xro, zpo, zro, fo, True)
    in_sum = Reduction(ri, cpi, ypi, xpi, xri, zpi, zri, fi, False)
    out_sum.go_core()

    for j in range(HALVES):
        wo = gout[16 * j : 16 * j + 16].reshape(HALF, C)
        ga = nn(gm[...], wo.T)
        gh[j] = (ga * slope[j]).astype(BF)
        part = nn(npt[...], gh[j]).astype(BF)
        for n in range(2):
            for c in range(2):
                ri[c, 2 * j + n] = part[192 * c : 192 * c + 192, C * n : C * (n + 1)]
        if j == 0:
            out_sum.go_y()
    in_sum.go_core()
    gn[...] = nn(gh[0], w_in[0].T) + nn(gh[1], w_in[1].T)
    in_sum.go_y()

    def norm_back(r, carry):
        cells = pl.ds(pl.multiple_of(r * COLS, COLS), COLS)
        unit = conv[r]
        g = gn[cells, :] * gain
        sp = spread_b[r]
        sp = jnp.concatenate([sp, sp, sp], axis=1)
        first = jnp.mean(g, axis=-1, keepdims=True)
        second = jnp.mean(g * unit, axis=-1, keepdims=True)
        gc = sp * (g - first - unit * second)
        gn[cells, :] = gc
        ghalf[r] = gc.astype(BF)
        return carry

    lax.fori_loop(0, ROWS, norm_back, 0)
    halo2 = halo_copies(ghalf, 1)
    begin(halo2)

    for t in range(TAPS * TAPS, 64):
        kp[t // 8, t % 8 : t % 8 + 1, :] = jnp.zeros((1, C), F32)

    def tap_sums(l, carry):
        for b in range(TAPS):
            def body(cg, acc, b=b):
                c0 = pl.multiple_of(cg * 8, 8)
                rows = [ext[l, row, pl.ds(c0 + 5 + b, 8), :] for row in range(ROWS + 2 * REACH)]
                acc = list(acc)
                for r in range(ROWS):
                    g = gn[pl.ds(c0 + COLS * r, 8), lanes(l)]
                    for a in range(TAPS):
                        acc[a] = acc[a] + g * rows[r + a]
                return tuple(acc)

            acc = lax.fori_loop(0, 16, body, (jnp.zeros((8, 128), F32),) * TAPS)
            for a in range(TAPS):
                t = a * TAPS + b
                kp[t // 8, t % 8 : t % 8 + 1, lanes(l)] = jnp.sum(acc[a], axis=0, keepdims=True)
        return carry

    lax.fori_loop(0, 2, tap_sums, 0)
    out_sum.go_x()
    lax.fori_loop(2, 3, tap_sums, 0)

    kz_c = [Copy(sems, kp.at[ring(z, k, NZ)], kz.at[k - 1], zdev(k)) for k in range(1, NZ)]
    kc_c = [Copy(sems, kcs, kc, other_core)]
    kx_c = [Copy(sems, kxs, kx.at[k - 1], xdev(k)) for k in range(1, NX)]
    ky_c = [Copy(sems, kys, ky.at[k - 1], ydev(k)) for k in range(1, NY)]
    kf_c = [
        Copy(sems, kf.at[z], kf.at[z], zdev(k), land=kf.at[ring(z, -k, NZ)]) for k in range(1, NZ)
    ]
    def arrive_all(copies):
        for c in copies:
            c.arrived()

    begin(kz_c)
    extend_own(ghalf, ext2)
    mixed[...] = nn(act[0], gout[0:16].reshape(HALF, C)) + nn(act[1], gout[16:32].reshape(HALF, C))
    for r in range(ROWS):
        row_scale = scale * flags[r]
        cells = pl.ds(COLS * r, COLS)
        new_ref[r] = (x_ref[r].astype(F32) + row_scale * mixed[cells, :]).astype(BF)
    arrive_all(halo2)
    extend_rim(1, ext2)
    in_sum.go_x()

    gs_part = conv
    stencil(ext2, True, gs_part, 0, 16)
    arrive_all(kz_c)
    total = kp[z]
    for n in range(NZ - 1):
        total = total + kz[n]
    kcs[...] = total
    begin(kc_c)
    out_sum.go_z()
    stencil(ext2, True, gs_part, 16, 24)
    arrive_all(kc_c)
    kxs[...] = kcs[...] + kc[...]
    begin(kx_c)
    stencil(ext2, True, gs_part, 24, 36)
    in_sum.go_z()
    stencil(ext2, True, gs_part, 36, 40)
    arrive_all(kx_c)
    kys[...] = kxs[...] + kx[0] + kx[1] + kx[2]
    begin(ky_c)
    stencil(ext2, True, gs_part, 40, 48)
    out_sum.go_gather()
    arrive_all(ky_c)
    kf[z] = (kys[...] + ky[0] + ky[1] + ky[2]) * NORM
    begin(kf_c)
    in_sum.go_gather()

    def finish_row(r, carry):
        gs_ref[r] = (cot_ref[r].astype(F32) + gs_part[r]).astype(BF)
        return carry

    lax.fori_loop(0, ROWS, finish_row, 0)
    out_sum.finish()
    for i in range(3):
        gwo_ref[16 * i : 16 * i + 16, :] = fo[i]
    in_sum.finish()
    for j in range(4):
        gwi_ref[:, C * j : C * (j + 1)] = fi[j, 0:12, :]
    arrive_all(kf_c)
    for n in range(6):
        gk_ref[8 * n : 8 * n + 8, :] = kf[n]
    gk_ref[48:49, :] = kf[6, 0:1, :]
    for c in started:
        c.left()


def per_device(
    ocean_state, kernel, norm_gain, weight_in, weight_out, layer_scale, cotangent, tile_list, ocean_count
):
    vmem = pl.BlockSpec(memory_space=pltpu.VMEM)
    smem = pl.BlockSpec(memory_space=pltpu.SMEM)
    V = pltpu.VMEM
    scratch = [
        V((2, 2, REACH, COLS, C), BF),
        V((2, 2, ROWS, 16, C), BF),
        V((2, 4, REACH, 16, C), BF),
        V((3, 14, 144, 128), F32),
        V((3, 14, 144, 128), F32),
        V((3, 49, 8, 128), F32),
        V((ROWS, COLS, C), F32),
        V((ROWS, COLS, 128), F32),
        V((ROWS * COLS, C), BF),
        V((C, ROWS * COLS), BF),
        V((ROWS * COLS, C), BF),
        V((ROWS, COLS, C), BF),
        V((3, 16, C), F32),
        V((32, 3, 16, C), BF),
        V((32, 48, C), BF),
        V((4, C, 512), BF),
        V((HALVES, C, HALF), BF),
        V((C, C), BF),
        V((HALVES, ROWS * COLS, HALF), BF),
        V((HALVES, ROWS * COLS, HALF), F32),
        V((HALVES, ROWS * COLS, HALF), BF),
        V((ROWS * COLS, C), F32),
        V((ROWS * COLS, C), F32),
        V((2, 3, 256, C), BF),
        V((2, 4, 192, C), BF),
        V((3, 256, C), BF),
        V((4, 192, C), BF),
        V((3, 256, C), BF),
        V((3, 192, C), BF),
        V((256, C), BF),
        V((192, C), BF),
        V((3, 128, C), BF),
        V((3, 96, C), BF),
        V((NZ, 16, C), BF),
        V((NZ, 16, C), BF),
        V((NZ - 1, 16, C), BF),
        V((NZ - 1, 16, C), BF),
        V((3, 16, C), F32),
        V((4, 16, C), F32),
        V((NZ, 8, C), F32),
        V((NZ - 1, 8, C), F32),
        V((8, C), F32),
        V((3, 8, C), F32),
        V((3, 8, C), F32),
        V((8, C), F32),
        V((8, C), F32),
        V((8, C), F32),
        V((NZ, 8, C), F32),
        pltpu.SemaphoreType.DMA((N_SEM,)),
        pltpu.SemaphoreType.DMA((N_SEM,)),
    ]
    return pl.pallas_call(
        kernel_body,
        out_shape=(
            jax.ShapeDtypeStruct((ROWS, COLS, C), BF),
            jax.ShapeDtypeStruct((ROWS, COLS, C), BF),
            jax.ShapeDtypeStruct((12, FF), F32),
            jax.ShapeDtypeStruct((48, C), F32),
            jax.ShapeDtypeStruct((TAPS * TAPS, C), F32),
        ),
        in_specs=[smem, smem] + [vmem] * 7,
        out_specs=(vmem,) * 5,
        scratch_shapes=scratch,
        compiler_params=pltpu.CompilerParams(
            collective_id=0, has_side_effects=True, vmem_limit_bytes=60 * 2**20
        ),
        cost_estimate=pl.CostEstimate(
            flops=8 * 10**9, bytes_accessed=4 * 10**6, transcendentals=4 * 10**6
        ),
        name="block",
    )(
        tile_list, ocean_count, ocean_state, kernel, norm_gain, weight_in, weight_out,
        layer_scale, cotangent,
    )


def solution(mesh):
    return jax.shard_map(
        per_device,
        mesh=mesh,
        in_specs=(
            P("lat", "lon", None),
            P(),
            P(),
            P("lat", None),
            P("lat", None),
            P(),
            P("lat", "lon", None),
            P("lat", "lon", None),
            P("lat", "lon"),
        ),
        out_specs=(
            P("lat", "lon", None),
            P("lat", "lon", None),
            P("lat", None),
            P("lat", None),
            P(),
        ),
        check_vma=False,
    )
```

time: 117 us -> 92.9 us (0.79)
  Pallas kernels: 108 us -> 84.7 us
  local copies, waits for them, and re-layouts: 7.42 us -> 5.6 us
    pallas_call x1, Pallas kernels: 108 us -> 84.7 us  [per_device(): pl.pallas_call(kernel_body, out_shape=(jax.ShapeDtypeStruct((ROWS, COLS,...]
    reshape x2 -> x0, local copies, waits for them, and re-layouts: 1.81 us -> none  [the longest x1 1.25 us: per_device(): norm_gain.reshape(1, C)]
    unnamed x15 -> x13, local copies, waits for them, and re-layouts: 5.61 us -> 5.6 us
where the time goes in v2:
time: 92.9 us; the launch traced here: 91.7 us
  Pallas kernels  84.7 us (91%)
  local copies, waits for them, and re-layouts  5.6 us (6%)
  between operations  1.3 us (1%)
    pallas_call x1, Pallas kernels, per_device(): pl.pallas_call(kernel_body, out_shape=(jax.ShapeDtypeStruct((ROWS, COLS,...  84.7 us
    unnamed x13, local copies, waits for them, and re-layouts  5.6 us

profile of v2, /device:TPU:32, one launch (start us, length us, event | category | flops | bytes accessed | tf_op | source)
XLA Modules:
  0.0 91.7 jit_solution(4682411466214799607)
XLA Ops:
  1.3 84.7 %block.1 = (bf16[8,128,384]{2,1,0:T(8,128)(2,1)}, bf16[8,128,384]{2,1,0:T(8,128)(2,1)}, f32[12,1536]{1,0:T(8,128)}, f32[48,384]{1,0:T(8,128)}, f32[49,384]{1,0:T(8,128)}) custom-call(s32[1,1,6]{2,1,0:T(1,128)} %tile_ref.1, s32[1,1]{1,0:T(1,128)S(6)} %copy.19.count_ref, bf16[8,128,384]{2,1,0:T(8,128)(2,1)} %x_ref.1, f32[49,384]{1,0:T(8,128)} %k_ref.1, ...), custom_call_target="tpu_custom_call" | custom-call | flops 8000000000 | bytes 4000000 | tf_op jit(solution)/shard_map/block/pallas_call | solution.py:707
  86.0 0.0 copy-start
  86.0 2.2 %copy.20 = bf16[8,128,384]{2,1,0:T(8,128)(2,1)} copy(bf16[8,128,384]{2,1,0:T(8,128)(2,1)} %get-tuple-element.10) | data formatting | bytes 1572864
  88.2 0.0 copy-done
  88.2 0.0 copy-start.1
  88.2 0.9 copy.21
  89.1 0.1 copy-done.1
  89.2 0.0 copy-start.3
  89.2 0.6 copy.22
  89.8 0.3 copy-done.3
  90.1 0.0 copy-start.2
  90.1 0.6 copy.23
  90.7 0.3 copy-done.2
  91.0 0.6 copy.24
Async XLA Ops:
  86.0 2.2 %copy-start = (bf16[8,128,384]{2,1,0:T(8,128)(2,1)S(1)}, bf16[8,128,384]{2,1,0:T(8,128)(2,1)}, u32[]{:S(2)}) copy-start(bf16[8,128,384]{2,1,0:T(8,128)(2,1)} %get-tuple-element.11) | copy-start | bytes 2359300
  88.2 1.0 %copy-start.1 = (f32[12,1536]{1,0:T(8,128)S(1)}, f32[12,1536]{1,0:T(8,128)}, u32[]{:S(2)}) copy-start(f32[12,1536]{1,0:T(8,128)} %get-tuple-element.12) | copy-start | bytes 221188
  89.2 0.9 %copy-start.3 = (f32[48,384]{1,0:T(8,128)S(1)}, f32[48,384]{1,0:T(8,128)}, u32[]{:S(2)}) copy-start(f32[48,384]{1,0:T(8,128)} %get-tuple-element.13) | copy-start | bytes 221188
  90.1 0.9 %copy-start.2 = (f32[49,384]{1,0:T(8,128)S(1)}, f32[49,384]{1,0:T(8,128)}, u32[]{:S(2)}) copy-start(f32[49,384]{1,0:T(8,128)} %get-tuple-element.14) | copy-start | bytes 225796

commit v3 on v2

--- a/solution.py
+++ b/solution.py
@@ -90,7 +90,7 @@
     hrow, hcol, hcor, ext, ext2, k8, conv, spread_b, normed, npt, gm, ghalf,
     pack, gin, gout, unpack, w_in, sel, act, slope, gh, mixed, gn,
     ro, ri, cpo, cpi, ypo, ypi, xpo, xpi, xro, xri, zpo, zpi, zro, zri, fo, fi,
-    kp, kz, kc, kx, ky, kcs, kxs, kys, kf,
+    kp, kz, kc, kxy, kcs, kcs2, kf,
     send, recv,
 ):
     lat, lon = lax.axis_index("lat"), lax.axis_index("lon")
@@ -117,6 +117,9 @@
 
     other_core = at(x, z, 1 - core, y)
 
+    def plane(i, j):
+        return at(ring(x, i, NX), z, core, ring(y, j, NY))
+
     def around(dr, dc):
         return (ring(lat, dr, 32), ring(lon, dc, 8))
 
@@ -126,6 +129,7 @@
     partners += [xdev(k) for k in range(1, NX)]
     partners += [ydev(k) for k in range(1, NY)]
     partners += [other_core]
+    partners += [plane(i, j) for i in range(1, NX) for j in range(1, NY)]
     for dev in partners:
         pl.semaphore_signal(barrier, inc=1, device_id=dev, device_id_type=MESH)
 
@@ -321,12 +325,12 @@
     extend_own(x_ref, ext)
     stencil_own(ext, conv, 0, 42)
     gather_in.onward(1, 7)
-    gather_out.launch()
     for c in halo1:
         c.arrived()
     extend_rim(0, ext)
     gather_in.onward(2, 6)
     gather_in.across(0)
+    gather_out.launch()
     stencil_rim(ext, conv)
     gather_in.onward(3, 5)
     gather_in.across(1, 7)
@@ -581,8 +585,8 @@
 
     kz_c = [Copy(sems, kp.at[ring(z, k, NZ)], kz.at[k - 1], zdev(k)) for k in range(1, NZ)]
     kc_c = [Copy(sems, kcs, kc, other_core)]
-    kx_c = [Copy(sems, kxs, kx.at[k - 1], xdev(k)) for k in range(1, NX)]
-    ky_c = [Copy(sems, kys, ky.at[k - 1], ydev(k)) for k in range(1, NY)]
+    steps = [(i, j) for i in range(NX) for j in range(NY) if i or j]
+    kp_c = [Copy(sems, kcs2, kxy.at[n], plane(*d)) for n, d in enumerate(steps)]
     kf_c = [
         Copy(sems, kf.at[z], kf.at[z], zdev(k), land=kf.at[ring(z, -k, NZ)]) for k in range(1, NZ)
     ]
@@ -612,19 +616,19 @@
     out_sum.go_z()
     stencil(ext2, True, gs_part, 16, 24)
     arrive_all(kc_c)
-    kxs[...] = kcs[...] + kc[...]
-    begin(kx_c)
+    kcs2[...] = kcs[...] + kc[...]
+    begin(kp_c)
     stencil(ext2, True, gs_part, 24, 36)
     in_sum.go_z()
-    stencil(ext2, True, gs_part, 36, 40)
-    arrive_all(kx_c)
-    kys[...] = kxs[...] + kx[0] + kx[1] + kx[2]
-    begin(ky_c)
-    stencil(ext2, True, gs_part, 40, 48)
+    stencil(ext2, True, gs_part, 36, 44)
+    arrive_all(kp_c)
+    total = kcs2[...]
+    for n in range(NX * NY - 1):
+        total = total + kxy[n]
+    kf[z] = total * NORM
+    begin(kf_c)
     out_sum.go_gather()
-    arrive_all(ky_c)
-    kf[z] = (kys[...] + ky[0] + ky[1] + ky[2]) * NORM
-    begin(kf_c)
+    stencil(ext2, True, gs_part, 44, 48)
     in_sum.go_gather()
 
     def finish_row(r, carry):
@@ -695,9 +699,7 @@
         V((NZ, 8, C), F32),
         V((NZ - 1, 8, C), F32),
         V((8, C), F32),
-        V((3, 8, C), F32),
-        V((3, 8, C), F32),
-        V((8, C), F32),
+        V((NX * NY - 1, 8, C), F32),
         V((8, C), F32),
         V((8, C), F32),
         V((NZ, 8, C), F32),

time: 92.9 us -> 91.7 us (0.987)
  no operation moved by 1% of the time
where the time goes in v3:
time: 91.7 us; the launch traced here: 90.7 us
  Pallas kernels  83.8 us (91%)
  local copies, waits for them, and re-layouts  5.6 us (6%)
  between operations  1.3 us (1%)
    pallas_call x1, Pallas kernels, per_device(): pl.pallas_call(kernel_body, out_shape=(jax.ShapeDtypeStruct((ROWS, COLS,...  83.8 us
    unnamed x13, local copies, waits for them, and re-layouts  5.6 us

profile of v3, /device:TPU:32, one launch (start us, length us, event | category | flops | bytes accessed | tf_op | source)
XLA Modules:
  0.0 90.7 jit_solution(12574134926883431690)
XLA Ops:
  1.3 83.8 %block.1 = (bf16[8,128,384]{2,1,0:T(8,128)(2,1)}, bf16[8,128,384]{2,1,0:T(8,128)(2,1)}, f32[12,1536]{1,0:T(8,128)}, f32[48,384]{1,0:T(8,128)}, f32[49,384]{1,0:T(8,128)}) custom-call(s32[1,1,6]{2,1,0:T(1,128)} %tile_ref.1, s32[1,1]{1,0:T(1,128)S(6)} %copy.19.count_ref, bf16[8,128,384]{2,1,0:T(8,128)(2,1)} %x_ref.1, f32[49,384]{1,0:T(8,128)} %k_ref.1, ...), custom_call_target="tpu_custom_call" | custom-call | flops 8000000000 | bytes 4000000 | tf_op jit(solution)/shard_map/block/pallas_call | solution.py:709
  85.1 0.0 copy-start
  85.1 2.2 %copy.20 = bf16[8,128,384]{2,1,0:T(8,128)(2,1)} copy(bf16[8,128,384]{2,1,0:T(8,128)(2,1)} %get-tuple-element.10) | data formatting | bytes 1572864
  87.3 0.0 copy-done
  87.3 0.0 copy-start.1
  87.3 0.9 copy.21
  88.2 0.1 copy-done.1
  88.3 0.0 copy-start.3
  88.3 0.6 copy.22
  88.9 0.3 copy-done.3
  89.2 0.0 copy-start.2
  89.2 0.6 copy.23
  89.8 0.3 copy-done.2
  90.1 0.6 copy.24
Async XLA Ops:
  85.1 2.2 %copy-start = (bf16[8,128,384]{2,1,0:T(8,128)(2,1)S(1)}, bf16[8,128,384]{2,1,0:T(8,128)(2,1)}, u32[]{:S(2)}) copy-start(bf16[8,128,384]{2,1,0:T(8,128)(2,1)} %get-tuple-element.11) | copy-start | bytes 2359300
  87.3 1.0 %copy-start.1 = (f32[12,1536]{1,0:T(8,128)S(1)}, f32[12,1536]{1,0:T(8,128)}, u32[]{:S(2)}) copy-start(f32[12,1536]{1,0:T(8,128)} %get-tuple-element.12) | copy-start | bytes 221188
  88.3 0.9 %copy-start.3 = (f32[48,384]{1,0:T(8,128)S(1)}, f32[48,384]{1,0:T(8,128)}, u32[]{:S(2)}) copy-start(f32[48,384]{1,0:T(8,128)} %get-tuple-element.13) | copy-start | bytes 221188
  89.2 0.9 %copy-start.2 = (f32[49,384]{1,0:T(8,128)S(1)}, f32[49,384]{1,0:T(8,128)}, u32[]{:S(2)}) copy-start(f32[49,384]{1,0:T(8,128)} %get-tuple-element.14) | copy-start | bytes 225796
